TPU v7x, 256 devices: a whole 4x4x8 slice. The times are simulated.
256 devices in a mesh: grp: 64 (over x, z_hi, y), tp: 4 (over z_lo, core).
Axes of the slice: x: 4, y: 4, z: 8 (z_hi: 4, z_lo: 2; z = z_hi * 2 + z_lo), core: 2. Of those that a mesh axis runs over, the one named last changes fastest.
Arguments:
- queries: bfloat16 [4, 128, 8192], P(None, 'grp')
- new_keys: bfloat16 [4, 128, 1024], P(None, 'grp'), may hold values from -6 to 6
- new_values: bfloat16 [4, 128, 1024], P(None, 'grp'), may hold values from -6 to 6
- key_cache: bfloat16 [64, 4, 6, 64, 1024], P('grp', 'tp'), may hold values from -6 to 6
- value_cache: bfloat16 [64, 4, 6, 64, 1024], P('grp', 'tp'), may hold values from -6 to 6
- page_table: int32 [128, 12], P('grp'), may hold values from 0 to 5, as said below
- context: int32 [128], P('grp'), may hold values from 1 to 764
- light_q: bfloat16 [4, 128, 8192], P(None, 'grp', 'tp'), may hold values from -6 to 6
- light_k: bfloat16 [4, 128, 8192], P(None, 'grp', 'tp'), may hold values from -0.5 to 0.5
- light_v: bfloat16 [4, 128, 8192], P(None, 'grp', 'tp'), may hold values from -6 to 6
- light_state: float32 [128, 64, 128, 128], P('grp', 'tp'), may hold values from -0.6 to 0.6
- decay_rate: float32 [64], P('tp'), may hold values from 0.01 to 1
- move_dist: int32 [2], replicated, may hold values from 1 to 63
- move_slot: int32 [2], replicated, may hold values from 0 to 1, as said below
Outputs:
- soft_mix: bfloat16 [4, 128, 8192], P(None, 'grp', 'tp')
- linear_mix: bfloat16 [4, 128, 8192], P(None, 'grp', 'tp')
- key_pages: bfloat16 [64, 4, 6, 64, 1024], P('grp', 'tp')
- value_pages: bfloat16 [64, 4, 6, 64, 1024], P('grp', 'tp')
- linear_states: float32 [128, 64, 128, 128], P('grp', 'tp')
- moved_table: int32 [128, 12], P('grp')
- moved_lengths: int32 [128], P('grp')
Inputs may be any that keep to these rules, and one draw needn't show every extreme that they name: `page_table`: slot i of a group owns pages i * 3 to i * 3 + 2 of each part; the row of a request lists, for each part, each of its pages once. `move_slot`: the sections name distinct slots.
All inputs are finite; a program needn't handle non-finite values.
Results may differ from a plain program's by a relative error of at most 0.017.
Values may be sent and summed in bfloat16 or wider, within the bound.
No kernel may reach another device: no remote copies, remote signals or barrier semaphores. Data moves between devices by JAX's collectives and lax.ppermute only.
A program may use at most 128 MiB of HBM per device.

v0:
```python
import functools

import jax
import jax.numpy as jnp
from jax import lax
from jax.experimental import pallas as pl
from jax.experimental.pallas import tpu as pltpu
from jax.sharding import PartitionSpec as P

MASKED_SCORE = -1e30
LANES = 128
META_ROWS = 16
DIMS0 = (((0,), (0,)), ((), ()))
DIMS1 = (((1,), (1,)), ((), ()))


def blocked(array):
    rank = len(array.shape)
    return pl.BlockSpec(array.shape, lambda i: (0,) * rank)


def scalars():
    return pl.BlockSpec(memory_space=pltpu.SMEM)


def cost(flops, moved, exps=0):
    return pl.CostEstimate(flops=flops, bytes_accessed=moved, transcendentals=exps)


def joined_rows(ref):
    value = ref[...].astype(jnp.float32)
    return jnp.concatenate([value[step] for step in range(value.shape[0])], axis=0)


def distance_of(slot, move_dist, move_slot):
    return jnp.where(move_slot[0] == slot, move_dist[0], move_dist[1])


def pieces(first, count, chunk):
    for at in range(first, first + count, 16):
        yield at - first, at // chunk, at % chunk


def rows_at(row):
    return pl.ds(pl.multiple_of(row, 16), 16)


def new_line(fresh, step, slot):
    value = fresh[step].astype(jnp.float32)
    return jnp.where(slot == 0, value[0:1], value[1:2])


def pack_kernel(
    table, context, decay, new_keys, new_values, key_cache, value_cache, light_k, light_v, state,
    send, rows_k, rows_v,
):
    slot = pl.program_id(0)
    steps, slots, width = new_keys.shape
    per_slot, page_len = key_cache.shape[2:4]
    heads = state.shape[1]
    kv_rows = per_slot * page_len
    kv_heads = width // LANES
    kv_all = 2 * kv_heads * kv_rows
    chunk = (send.shape[1] - META_ROWS) // slots
    begin = slot * chunk
    tp_rank, tp_count = lax.axis_index("tp"), lax.axis_size("tp")
    halves = ((new_keys, key_cache, 0), (new_values, value_cache, kv_heads * kv_rows))

    for _, cache, first in halves:
        for head in range(kv_heads):
            over = slice(head * LANES, (head + 1) * LANES)
            for at, place, here in pieces(first + head * kv_rows, kv_rows, chunk):
                page, row = divmod(at, page_len)
                send[place, rows_at(begin + here), :] = cache[0, 0, page, row : row + 16, over]
    for step in range(steps):
        place = context[slot] + step
        logical = place // page_len

        @pl.when(logical % tp_count == tp_rank)
        def _():
            row = (table[slot, logical] - slot * per_slot) * page_len + place % page_len
            base = row // 16 * 16
            hit = lax.broadcasted_iota(jnp.int32, (16, LANES), 0) == row - base
            for fresh, _, first in halves:
                line = new_line(fresh, step, slot)
                for head in range(kv_heads):
                    at = first + head * kv_rows + base
                    here = rows_at(begin + at % chunk)
                    old = send[at // chunk, here, :].astype(jnp.float32)
                    new = line[:, head * LANES : (head + 1) * LANES]
                    send[at // chunk, here, :] = jnp.where(hit, new, old).astype(jnp.bfloat16)

    @pl.when(slot == 0)
    def _():
        rows_k[...] = joined_rows(light_k)
        rows_v[...] = joined_rows(light_v)
        line = lax.broadcasted_iota(jnp.int32, (META_ROWS, LANES), 0)
        lane = lax.broadcasted_iota(jnp.int32, (META_ROWS, LANES), 1)
        numbers = jnp.zeros((META_ROWS, LANES), jnp.int32)
        for owner in range(slots):
            entries = [table[owner, logical] for logical in range(table.shape[1])]
            entries += [context[owner] // 256, context[owner] % 256]
            for index, entry in enumerate(entries):
                numbers = jnp.where((line == owner) & (lane == index), entry, numbers)
        numbers = numbers.astype(jnp.float32).astype(jnp.bfloat16)
        for place in range(send.shape[0]):
            send[place, slots * chunk :, :] = numbers

    row = lax.broadcasted_iota(jnp.int32, (steps * slots, LANES), 0)
    age = (steps - 1 - row // slots).astype(jnp.float32)
    mine = row % slots == slot
    for head in range(heads):
        lanes = slice(head * LANES, (head + 1) * LANES)
        rate = decay[head]
        aged = jnp.where(mine, rows_k[:, lanes] * jnp.exp(-age * rate), 0.0)
        added = lax.dot_general(
            aged.astype(jnp.bfloat16),
            rows_v[:, lanes].astype(jnp.bfloat16),
            DIMS0,
            preferred_element_type=jnp.float32,
        )
        fade = jnp.exp(jnp.full((1, LANES), -float(steps), jnp.float32) * rate)
        final = (state[0, head] * fade + added).astype(jnp.bfloat16)
        for at, place, here in pieces(kv_all + head * LANES, LANES, chunk):
            send[place, rows_at(begin + here), :] = final[at : at + 16]


def linear_kernel(
    decay, light_q, light_k, light_v, state, linear_mix, rows_q, rows_k, rows_v, rows_out
):
    slots, heads = state.shape[:2]
    steps = light_q.shape[0]
    rows_q[...] = joined_rows(light_q)
    rows_k[...] = joined_rows(light_k)
    rows_v[...] = joined_rows(light_v)
    rows = steps * slots
    row = lax.broadcasted_iota(jnp.int32, (rows, LANES), 0)
    step_of = (row // slots).astype(jnp.float32)
    first = row % slots == 0
    pair_row = lax.broadcasted_iota(jnp.int32, (rows, rows), 0)
    pair_col = lax.broadcasted_iota(jnp.int32, (rows, rows), 1)
    gap = pair_row // slots - pair_col // slots
    counted = (pair_row % slots == pair_col % slots) & (gap >= 0)
    gap = jnp.maximum(gap, 0).astype(jnp.float32)
    for head in range(heads):
        lanes = slice(head * LANES, (head + 1) * LANES)
        rate = decay[head]
        q16, k16, v16 = (part[:, lanes].astype(jnp.bfloat16) for part in (rows_q, rows_k, rows_v))
        both = [state[slot, head].astype(jnp.bfloat16) for slot in range(slots)]
        base = jnp.dot(q16, jnp.concatenate(both, axis=1), preferred_element_type=jnp.float32)
        base = jnp.where(first, base[:, :LANES], base[:, LANES:])
        base = base * jnp.exp(-(step_of + 1.0) * rate)
        match = lax.dot_general(q16, k16, DIMS1, preferred_element_type=jnp.float32)
        match = jnp.where(counted, match * jnp.exp(-gap * rate), 0.0)
        recent = jnp.dot(match.astype(jnp.bfloat16), v16, preferred_element_type=jnp.float32)
        rows_out[:, lanes] = base + recent
    for step in range(steps):
        linear_mix[step] = rows_out[step * slots : (step + 1) * slots, :].astype(jnp.bfloat16)


def thirds(value):
    high = value.astype(jnp.bfloat16)
    rest = value - high.astype(jnp.float32)
    middle = rest.astype(jnp.bfloat16)
    low = (rest - middle.astype(jnp.float32)).astype(jnp.bfloat16)
    return [part.astype(jnp.float32) for part in (high, middle, low)]


def attend_kernel(
    table, context, queries, new_keys, new_values, key_cache, value_cache, *rest
):
    *sends, pack_0, pack_1, rows_q = rest
    steps, slots, width = new_keys.shape
    page_len = key_cache.shape[3]
    per_slot = key_cache.shape[2] // slots
    kv_rows = per_slot * page_len
    kv_heads = width // LANES
    share = queries.shape[2] // width
    rows = steps * slots
    tp_rank, tp_count = lax.axis_index("tp"), lax.axis_size("tp")
    packs = (pack_0, pack_1)
    halves = ((new_keys, key_cache, 0), (new_values, value_cache, kv_heads * kv_rows))

    for slot in range(slots):
        pack = packs[slot]
        for _, cache, first in halves:
            for page in range(per_slot):
                for head in range(kv_heads):
                    at = first + head * kv_rows + page * page_len
                    over = slice(head * LANES, (head + 1) * LANES)
                    pack[at : at + page_len, :] = cache[0, 0, slot * per_slot + page, :, over]
        for step in range(steps):
            place = context[slot] + step
            logical = place // page_len

            @pl.when(logical % tp_count == tp_rank)
            def _():
                row = (table[slot, logical] - slot * per_slot) * page_len + place % page_len
                base = row // 16 * 16
                hit = lax.broadcasted_iota(jnp.int32, (16, LANES), 0) == row - base
                for fresh, _, first in halves:
                    line = new_line(fresh, step, slot)
                    for head in range(kv_heads):
                        here = pl.ds(pl.multiple_of(first + head * kv_rows + base, 16), 16)
                        old = pack[here, :].astype(jnp.float32)
                        new = line[:, head * LANES : (head + 1) * LANES]
                        pack[here, :] = jnp.where(hit, new, old).astype(jnp.bfloat16)

    rows_q[...] = joined_rows(queries)
    count = share * rows
    row = lax.broadcasted_iota(jnp.int32, (count, kv_rows), 0) % rows
    column = lax.broadcasted_iota(jnp.int32, (count, kv_rows), 1)
    limits = []
    for slot in range(slots):
        base = jnp.zeros((count, kv_rows), jnp.int32)
        for page in range(per_slot):
            number = slot * per_slot + page
            logical = 0
            for turn in range(per_slot):
                guess = turn * tp_count + tp_rank
                logical = logical + jnp.where(table[slot, guess] == number, guess, 0)
            base = jnp.where(column // page_len == page, logical * page_len, base)
        limits.append(context[slot] + row // slots - base - column % page_len)
    first = row % slots == 0
    visible = jnp.where(first, limits[0], limits[1]) >= 0
    first_out = first[:, :LANES]
    lane = lax.broadcasted_iota(jnp.int32, (count, LANES), 1)
    scale = float(LANES) ** -0.5
    per_part = kv_heads // tp_count
    for turn in range(tp_count):
        target = jnp.bitwise_xor(tp_rank, turn)
        for half in range(per_part):
            head = target * per_part + half
            query = jnp.concatenate(
                [
                    rows_q[:, pl.ds(pl.multiple_of((head * share + one) * LANES, LANES), LANES)]
                    for one in range(share)
                ],
                axis=0,
            ).astype(jnp.bfloat16)
            key_at = pl.ds(pl.multiple_of(head * kv_rows, 16), kv_rows)
            value_at = pl.ds(pl.multiple_of((kv_heads + head) * kv_rows, 16), kv_rows)
            scores = [
                lax.dot_general(query, pack[key_at, :], DIMS1, preferred_element_type=jnp.float32)
                for pack in packs
            ]
            scores = jnp.where(visible, jnp.where(first, *scores) * scale, MASKED_SCORE)
            top = jnp.max(scores, axis=-1, keepdims=True)
            weights = jnp.where(visible, jnp.exp(scores - top), 0.0)
            total = jnp.sum(weights, axis=-1, keepdims=True)
            weights = weights.astype(jnp.bfloat16)
            mixed = [
                jnp.dot(weights, pack[value_at, :], preferred_element_type=jnp.float32)
                for pack in packs
            ]
            at = slice(half * count, (half + 1) * count)
            sends[turn][at, :LANES] = jnp.where(first_out, *mixed).astype(jnp.bfloat16)
            extra = jnp.zeros((count, LANES), jnp.float32)
            for index, part in enumerate(thirds(top) + thirds(total)):
                extra = jnp.where(lane == index, part, extra)
            sends[turn][at, LANES:] = extra.astype(jnp.bfloat16)


def merge_kernel(*refs):
    parts, soft_mix, rows_out = refs[:-2], refs[-2], refs[-1]
    steps, slots, width = soft_mix.shape
    rows = steps * slots
    tops, totals = [], []
    for part in parts:
        extra = part[:, LANES:].astype(jnp.float32)
        tops.append(extra[:, 0:1] + extra[:, 1:2] + extra[:, 2:3])
        totals.append(extra[:, 3:4] + extra[:, 4:5] + extra[:, 5:6])
    peak = functools.reduce(jnp.maximum, tops)
    scales = [jnp.exp(top - peak) for top in tops]
    total = sum(total * scale for total, scale in zip(totals, scales))
    mixed = sum(part[:, :LANES].astype(jnp.float32) * scale for part, scale in zip(parts, scales))
    mixed = mixed / total
    for one in range(width // LANES):
        rows_out[:, one * LANES : (one + 1) * LANES] = mixed[one * rows : (one + 1) * rows]
    for step in range(steps):
        soft_mix[step] = rows_out[step * slots : (step + 1) * slots, :].astype(jnp.bfloat16)


def roll_kernel(slots, move_dist, move_slot, source, target):
    count = source.shape[0]
    chunk = target.shape[1] // slots
    for slot in range(slots):
        here = slice(slot * chunk, (slot + 1) * chunk)
        distance = distance_of(slot, move_dist, move_slot)

        def step(at, _):
            target[lax.rem(at + distance, count), here, :] = source[at, here, :]
            return 0

        lax.fori_loop(0, count, step, 0, unroll=4)


def unpack_kernel(
    steps, move_dist, move_slot, metas, landed, keys, values, states, table, lengths
):
    slot = pl.program_id(0)
    heads = states.shape[1]
    per_slot, page_len, width = keys.shape[2:]
    kv_rows = per_slot * page_len
    kv_heads = width // LANES
    entries = table.shape[1]
    group, count = lax.axis_index("grp"), lax.axis_size("grp")
    chunk = landed.shape[1]
    for pages, first in ((keys, 0), (values, kv_heads * kv_rows)):
        for head in range(kv_heads):
            over = slice(head * LANES, (head + 1) * LANES)
            for at, place, here in pieces(first + head * kv_rows, kv_rows, chunk):
                page, row = divmod(at, page_len)
                pages[0, 0, page, row : row + 16, over] = landed[place, here : here + 16, :]
    for head in range(heads):
        first = 2 * kv_heads * kv_rows + head * LANES
        for at, place, here in pieces(first, LANES, chunk):
            states[0, head, at : at + 16, :] = landed[place, here : here + 16, :].astype(jnp.float32)
    source = lax.rem(group - distance_of(slot, move_dist, move_slot) + count, count)
    meta = metas[source].astype(jnp.float32)
    meta = jnp.where(slot == 0, meta[0:1], meta[1:2])
    row = lax.broadcasted_iota(jnp.int32, table.shape, 0)
    table[...] = jnp.where(row == slot, meta[:, :entries].astype(jnp.int32), table[...])
    lane = lax.broadcasted_iota(jnp.int32, meta.shape, 1)
    weight = jnp.where(lane == entries, 256.0, jnp.where(lane == entries + 1, 1.0, 0.0))
    length = jnp.sum(meta * weight)
    lengths[slot] = length.astype(jnp.int32) + steps


def exchanged(value):
    return lax.all_to_all(value, "grp", 0, 0, tiled=True)


def by_slot(array, axis, slots):
    shape = tuple(size // slots if at == axis else size for at, size in enumerate(array.shape))
    return pl.BlockSpec(shape, lambda i: tuple(i if at == axis else 0 for at in range(len(shape))))


def called(kernel, out_shape, args, in_specs, out_specs, estimate, name, scratch=(), grid=1, vmem=32):
    return pl.pallas_call(
        kernel,
        grid=(grid,),
        out_shape=out_shape,
        in_specs=in_specs,
        out_specs=out_specs,
        scratch_shapes=list(scratch),
        compiler_params=pltpu.CompilerParams(vmem_limit_bytes=vmem * 1024 * 1024),
        cost_estimate=estimate,
        name=name,
    )(*args)


def per_device(
    queries,
    new_keys,
    new_values,
    key_cache,
    value_cache,
    page_table,
    context,
    light_q,
    light_k,
    light_v,
    light_state,
    decay_rate,
    move_dist,
    move_slot,
):
    steps, slots, width = new_keys.shape
    page_len = key_cache.shape[3]
    per_slot = key_cache.shape[2] // slots
    heads = light_state.shape[1]
    kv_all = 2 * per_slot * page_len * width // LANES
    tp_count, groups = lax.axis_size("tp"), lax.axis_size("grp")
    rows = steps * slots
    shape = jax.ShapeDtypeStruct
    line = pltpu.VMEM((rows, heads * LANES), jnp.float32)
    chunk = (kv_all + heads * LANES) // groups
    send_all = shape((groups, slots * chunk, LANES), jnp.bfloat16)

    first_all = shape((groups, slots * chunk + META_ROWS, LANES), jnp.bfloat16)

    send = called(
        pack_kernel,
        first_all,
        (
            page_table, context, decay_rate, new_keys, new_values, key_cache, value_cache,
            light_k, light_v, light_state,
        ),
        [scalars()] * 3
        + [blocked(new_keys), blocked(new_values)]
        + [by_slot(key_cache, 2, slots), by_slot(value_cache, 2, slots)]
        + [blocked(light_k), blocked(light_v), by_slot(light_state, 0, slots)],
        blocked(first_all),
        cost(1 << 24, 7 << 20),
        "pack",
        [line] * 2,
        slots,
        60,
    )
    spread = exchanged(send)

    linear_mix = called(
        linear_kernel,
        shape(light_q.shape, jnp.bfloat16),
        (decay_rate, light_q, light_k, light_v, light_state),
        [scalars()] + [blocked(arg) for arg in (light_q, light_k, light_v, light_state)],
        blocked(light_q),
        cost(1 << 24, 3 << 20),
        "linear",
        [line] * 4,
    )

    send_rows = rows * queries.shape[2] // LANES // tp_count
    send_shape = shape((send_rows, 2 * LANES), jnp.bfloat16)
    attended = (queries, new_keys, new_values, key_cache, value_cache)
    sends = called(
        attend_kernel,
        (send_shape,) * tp_count,
        (page_table, context, *attended),
        [scalars()] * 2 + [blocked(arg) for arg in attended],
        (blocked(send_shape),) * tp_count,
        cost(1 << 28, 2 << 20, 1 << 18),
        "attend",
        [pltpu.VMEM((kv_all, LANES), jnp.bfloat16)] * slots
        + [pltpu.VMEM((rows, queries.shape[2]), jnp.float32)],
    )
    received = [sends[0]] + [
        lax.ppermute(sends[turn], "tp", [(at, at ^ turn) for at in range(tp_count)])
        for turn in range(1, tp_count)
    ]

    turned = called(
        functools.partial(roll_kernel, slots),
        send_all,
        (move_dist, move_slot, spread),
        [scalars()] * 2 + [blocked(first_all)],
        blocked(send_all),
        cost(1 << 10, 5 << 20),
        "roll",
    )
    landed = exchanged(turned)

    mixed = shape((steps, slots, heads * LANES), jnp.bfloat16)
    soft_mix = called(
        merge_kernel,
        mixed,
        tuple(received),
        [blocked(send_shape)] * tp_count,
        blocked(mixed),
        cost(1 << 20, 1 << 18, 1 << 10),
        "merge",
        [line],
    )
    outs = (
        shape(key_cache.shape, jnp.bfloat16),
        shape(value_cache.shape, jnp.bfloat16),
        shape(light_state.shape, jnp.float32),
        shape(page_table.shape, jnp.int32),
        shape(context.shape, jnp.int32),
    )
    metas = pl.BlockSpec((groups, META_ROWS, LANES), lambda i: (0, slots * chunk // META_ROWS, 0))
    keys, values, states, table, lengths = called(
        functools.partial(unpack_kernel, steps),
        outs,
        (move_dist, move_slot, spread, landed),
        [scalars()] * 2 + [metas, by_slot(send_all, 1, slots)],
        (
            by_slot(outs[0], 2, slots), by_slot(outs[1], 2, slots), by_slot(outs[2], 0, slots),
            blocked(outs[3]), scalars(),
        ),
        cost(1 << 20, 6 << 20),
        "unpack",
        (),
        slots,
    )
    return soft_mix, linear_mix, keys, values, states, table, lengths


def solution(mesh):
    placed = (
        P(None, "grp", None),
        P(None, "grp", None),
        P(None, "grp", None),
        P("grp", "tp", None, None, None),
        P("grp", "tp", None, None, None),
        P("grp", None),
        P("grp"),
        P(None, "grp", "tp"),
        P(None, "grp", "tp"),
        P(None, "grp", "tp"),
        P("grp", "tp", None, None),
        P("tp"),
        P(),
        P(),
    )
    return jax.shard_map(
        per_device,
        mesh=mesh,
        in_specs=placed,
        out_specs=(
            P(None, "grp", "tp"),
            P(None, "grp", "tp"),
            P("grp", "tp", None, None, None),
            P("grp", "tp", None, None, None),
            P("grp", "tp", None, None),
            P("grp", None),
            P("grp"),
        ),
        check_vma=False,
    )
```

profile of v0, /device:TPU:8, one launch (start us, length us, event | category | flops | bytes accessed | tf_op | source)
XLA Modules:
  0.0 158.9 jit_solution(7023179176980519150)
XLA Ops:
  0.6 4.9 %pack.1 = bf16[64,176,128]{2,1,0:T(8,128)(2,1)} custom-call(s32[2,12]{1,0:T(2,128)} %table.3, s32[2]{0:T(128)} %context.3, f32[16]{0:T(128)} %decay.3, bf16[4,2,1024]{2,1,0:T(2,128)(2,1)} %new_keys.3, bf16[4,2,1024]{2,1,0:T(2,128)(2,1)} %new_values.3, bf16[1,1,6,64,1024]{4,3,2,1,0:T(8,128)(2,1)} %key_cache.3, bf16[1,1,6,64,1024]{4,3,2,1,0:T(8,128)(2,1)} %value_cache.3, ...), custom_call_target="tpu_custom_call" | custom-call | flops 16777216 | bytes 7340032 | tf_op jit(solution)/shard_map/pack/pallas_call | solution.py:340
  5.5 75.1 %all_to_all.10.source.metas = bf16[64,176,128]{2,1,0:T(8,128)(2,1)S(1)} all-to-all(bf16[64,176,128]{2,1,0:T(8,128)(2,1)} %pack.1), channel_id=1, replica_groups=mesh['grp'=64,'tp'=4] {'grp'}, dimensions={0} | all-to-all | bytes 5767168 | tf_op jit(solution)/shard_map/all_to_all | solution.py:331
  80.7 1.1 roll.1
  81.8 1.5 copy-done
  83.3 0.0 copy-start.11
  83.3 0.0 copy-start.4
  83.3 0.0 copy-start.5
  83.3 0.0 copy-start.9
  83.3 0.0 copy-start.12
  83.3 12.2 %all-to-all-start.1 = ((bf16[64,160,128]{2,1,0:T(8,128)(2,1)}), bf16[64,160,128]{2,1,0:T(8,128)(2,1)}, u32[]{:S(2)}, u32[]{:S(2)}) async-start(bf16[64,160,128]{2,1,0:T(8,128)(2,1)} %copy-done), calls=%async_computation.1 | async-start | bytes 5242880 | tf_op jit(solution)/shard_map/all_to_all | solution.py:331
  95.6 0.0 copy-start.2
  95.6 1.1 copy-done.2
  96.8 1.1 copy-done.3
  97.9 3.6 %attend.1 = (bf16[128,256]{1,0:T(8,128)(2,1)S(1)}, bf16[128,256]{1,0:T(8,128)(2,1)S(1)}, bf16[128,256]{1,0:T(8,128)(2,1)S(1)}, bf16[128,256]{1,0:T(8,128)(2,1)S(1)}) custom-call(s32[2,12]{1,0:T(2,128)S(1)} %copy-done.10, s32[2]{0:T(128)S(1)} %copy-done.11, bf16[4,2,8192]{2,1,0:T(2,128)(2,1)S(1)} %copy-done.6, bf16[4,2,1024]{2,1,0:T(2,128)(2,1)S(1)} %copy-done.7, ...), custom_call_target="tpu_custom_call" | custom-call | flops 268435456 | bytes 2097152 | tf_op jit(solution)/shard_map/attend/pallas_call | solution.py:340
  101.5 0.1 collective-permute-start
  101.6 6.3 %collective-permute-start.1 = (bf16[128,256]{1,0:T(8,128)(2,1)S(1)}, bf16[128,256]{1,0:T(8,128)(2,1)S(1)}, u32[]{:S(2)}, u32[]{:S(2)}) collective-permute-start(bf16[128,256]{1,0:T(8,128)(2,1)S(1)} %get-tuple-element.18), channel_id=1, source_target_pairs={{0,2},{1,3},{2,0},{3,1},{4,6},{5,7},{6,4},{7,5},{8,10},{9,11},{10,... | collective-permute-start | bytes 196616 | tf_op jit(solution)/shard_map/ppermute | solution.py:429
  107.9 0.1 collective-permute-start.2
  108.0 1.6 copy-done.1
  109.6 2.4 %linear.1 = bf16[4,2,2048]{2,1,0:T(2,128)(2,1)} custom-call(f32[16]{0:T(128)S(1)} %copy-done.12, bf16[4,2,2048]{2,1,0:T(2,128)(2,1)S(1)} %copy-done.9, bf16[4,2,2048]{2,1,0:T(2,128)(2,1)S(1)} %copy-done.4, bf16[4,2,2048]{2,1,0:T(2,128)(2,1)S(1)} %copy-done.5, f32[2,16,128,128]{3,2,1,0:T(8,128)S(1)} %copy-done.1), custom_call_target="tpu_custom_call" | custom-call | flops 16777216 | bytes 3145728 | tf_op jit(solution)/shard_map/linear/pallas_call | solution.py:340
  112.0 39.7 %collective-permute-done.1.refs_2_ = bf16[128,256]{1,0:T(8,128)(2,1)S(1)} collective-permute-done((bf16[128,256]{1,0:T(8,128)(2,1)S(1)}, bf16[128,256]{1,0:T(8,128)(2,1)S(1)}, u32[]{:S(2)}, u32[]{:S(2)}) %collective-permute-start.1) | collective-permute-done | bytes 65568 | tf_op jit(solution)/shard_map/ppermute | solution.py:429
  151.7 1.5 collective-permute-done.2.refs_3_
  153.2 1.1 merge.1
  154.3 1.2 all-to-all-done.1.landed
  155.4 3.5 %unpack.1 = (bf16[1,1,6,64,1024]{4,3,2,1,0:T(8,128)(2,1)}, bf16[1,1,6,64,1024]{4,3,2,1,0:T(8,128)(2,1)}, f32[2,16,128,128]{3,2,1,0:T(8,128)}, s32[2,12]{1,0:T(2,128)}, s32[2]{0:T(128)}) custom-call(s32[2]{0:T(128)S(1)} %copy-done.13, s32[2]{0:T(128)S(1)} %copy-done.14, bf16[64,176,128]{2,1,0:T(8,128)(2,1)S(1)} %all_to_all.10.source.metas, ...), custom_call_target="tpu_custom_call" | custom-call | flops 1048576 | bytes 6291456 | tf_op jit(solution)/shard_map/unpack/pallas_call | solution.py:340
  (21 shorter events, 0.0 us)
Async XLA Ops:
  5.5 75.2 %copy-start.13 = (s32[2]{0:T(128)S(1)}, s32[2]{0:T(128)}, u32[]{:S(2)}) copy-start(s32[2]{0:T(128)} %move_dist.3) | copy-start | bytes 28
  5.5 75.2 %copy-start.14 = (s32[2]{0:T(128)S(1)}, s32[2]{0:T(128)}, u32[]{:S(2)}) copy-start(s32[2]{0:T(128)} %move_slot.3) | copy-start | bytes 28
  81.7 1.5 copy-start
  83.3 12.3 %copy-start.6 = (bf16[4,2,8192]{2,1,0:T(2,128)(2,1)S(1)}, bf16[4,2,8192]{2,1,0:T(2,128)(2,1)}, u32[]{:S(2)}) copy-start(bf16[4,2,8192]{2,1,0:T(2,128)(2,1)} %queries.1) | copy-start | bytes 393220
  83.3 12.3 %copy-start.7 = (bf16[4,2,1024]{2,1,0:T(2,128)(2,1)S(1)}, bf16[4,2,1024]{2,1,0:T(2,128)(2,1)}, u32[]{:S(2)}) copy-start(bf16[4,2,1024]{2,1,0:T(2,128)(2,1)} %new_keys.3) | copy-start | bytes 49156
  83.3 12.3 %copy-start.8 = (bf16[4,2,1024]{2,1,0:T(2,128)(2,1)S(1)}, bf16[4,2,1024]{2,1,0:T(2,128)(2,1)}, u32[]{:S(2)}) copy-start(bf16[4,2,1024]{2,1,0:T(2,128)(2,1)} %new_values.3) | copy-start | bytes 49156
  83.3 12.3 %copy-start.10 = (s32[2,12]{1,0:T(2,128)S(1)}, s32[2,12]{1,0:T(2,128)}, u32[]{:S(2)}) copy-start(s32[2,12]{1,0:T(2,128)} %table.3) | copy-start | bytes 292
  83.3 12.3 %copy-start.11 = (s32[2]{0:T(128)S(1)}, s32[2]{0:T(128)}, u32[]{:S(2)}) copy-start(s32[2]{0:T(128)} %context.3) | copy-start | bytes 28
  83.3 24.7 %copy-start.4 = (bf16[4,2,2048]{2,1,0:T(2,128)(2,1)S(1)}, bf16[4,2,2048]{2,1,0:T(2,128)(2,1)}, u32[]{:S(2)}) copy-start(bf16[4,2,2048]{2,1,0:T(2,128)(2,1)} %light_k.3) | copy-start | bytes 98308
  83.3 24.7 %copy-start.5 = (bf16[4,2,2048]{2,1,0:T(2,128)(2,1)S(1)}, bf16[4,2,2048]{2,1,0:T(2,128)(2,1)}, u32[]{:S(2)}) copy-start(bf16[4,2,2048]{2,1,0:T(2,128)(2,1)} %light_v.3) | copy-start | bytes 98308
  83.3 24.6 %copy-start.9 = (bf16[4,2,2048]{2,1,0:T(2,128)(2,1)S(1)}, bf16[4,2,2048]{2,1,0:T(2,128)(2,1)}, u32[]{:S(2)}) copy-start(bf16[4,2,2048]{2,1,0:T(2,128)(2,1)} %light_q.1) | copy-start | bytes 98308
  83.3 24.6 %copy-start.12 = (f32[16]{0:T(128)S(1)}, f32[16]{0:T(128)}, u32[]{:S(2)}) copy-start(f32[16]{0:T(128)} %decay.3) | copy-start | bytes 196
  83.3 72.1 %all-to-all-start.1 = ((bf16[64,160,128]{2,1,0:T(8,128)(2,1)}), bf16[64,160,128]{2,1,0:T(8,128)(2,1)}, u32[]{:S(2)}, u32[]{:S(2)}) async-start(bf16[64,160,128]{2,1,0:T(8,128)(2,1)} %copy-done), calls=%async_computation.1 | async-start | bytes 5242880 | tf_op jit(solution)/shard_map/all_to_all | solution.py:331
  95.6 1.1 copy-start.2
  96.8 1.1 copy-start.3
  101.5 10.5 %collective-permute-start = (bf16[128,256]{1,0:T(8,128)(2,1)S(1)}, bf16[128,256]{1,0:T(8,128)(2,1)S(1)}, u32[]{:S(2)}, u32[]{:S(2)}) collective-permute-start(bf16[128,256]{1,0:T(8,128)(2,1)S(1)} %get-tuple-element.17), channel_id=1, source_target_pairs={{0,1},{1,0},{2,3},{3,2},{4,5},{5,4},{6,7},{7,6},{8,9},{9,8},{10,11... | collective-permute-start | bytes 196616 | tf_op jit(solution)/shard_map/ppermute | solution.py:429
  101.6 50.1 %collective-permute-start.1 = (bf16[128,256]{1,0:T(8,128)(2,1)S(1)}, bf16[128,256]{1,0:T(8,128)(2,1)S(1)}, u32[]{:S(2)}, u32[]{:S(2)}) collective-permute-start(bf16[128,256]{1,0:T(8,128)(2,1)S(1)} %get-tuple-element.18), channel_id=1, source_target_pairs={{0,2},{1,3},{2,0},{3,1},{4,6},{5,7},{6,4},{7,5},{8,10},{9,11},{10,... | collective-permute-start | bytes 196616 | tf_op jit(solution)/shard_map/ppermute | solution.py:429
  107.9 45.3 %collective-permute-start.2 = (bf16[128,256]{1,0:T(8,128)(2,1)S(1)}, bf16[128,256]{1,0:T(8,128)(2,1)S(1)}, u32[]{:S(2)}, u32[]{:S(2)}) collective-permute-start(bf16[128,256]{1,0:T(8,128)(2,1)S(1)} %get-tuple-element.19), channel_id=1, source_target_pairs={{0,3},{1,2},{2,1},{3,0},{4,7},{5,6},{6,5},{7,4},{8,11},{9,10},{10,... | collective-permute-start | bytes 196616 | tf_op jit(solution)/shard_map/ppermute | solution.py:429
  108.0 1.6 %copy-start.1 = (f32[2,16,128,128]{3,2,1,0:T(8,128)S(1)}, f32[2,16,128,128]{3,2,1,0:T(8,128)}, u32[]{:S(2)}) copy-start(f32[2,16,128,128]{3,2,1,0:T(8,128)} %state.3) | copy-start | bytes 6291460
where the time goes:
time: 162 us; the launch traced here: 159 us
  blocking collectives  75.1 us (46%)
  waiting for transfers between devices  42.4 us (26%)
  starting transfers between devices  18.7 us (12%)
  Pallas kernels  16.4 us (10%)
  local copies, waits for them, and re-layouts  5.42 us (3%)
    all_to_all x1, blocking collectives, exchanged(): return lax.all_to_all(value, 'grp', 0, 0, tiled=True)  75.1 us
    ppermute x3, waiting for transfers between devices, per_device(): lax.ppermute(sends[turn], 'tp', [(at, at ^ turn) for at in range(tp_count)])  41.2 us
    pallas_call x6, Pallas kernels, called(): pl.pallas_call(kernel, grid=(grid,), out_shape=out_shape, in_specs=in_spe...  16.4 us
    all_to_all x1, starting transfers between devices, exchanged(): return lax.all_to_all(value, 'grp', 0, 0, tiled=True)  12.2 us
    ppermute x3, starting transfers between devices, per_device(): lax.ppermute(sends[turn], 'tp', [(at, at ^ turn) for at in range(tp_count)])  6.47 us
    unnamed x30, local copies, waits for them, and re-layouts  5.42 us
  transfers between devices with their start and end apart: 4, of which 3 were waited for; matrix products, arithmetic and copies ran while one was open for 0% of the time, Pallas kernels for 4%

commit v1 on v0

--- a/solution.py
+++ b/solution.py
@@ -9,7 +9,8 @@
 
 MASKED_SCORE = -1e30
 LANES = 128
-META_ROWS = 16
+META_ROWS = 8
+ROLL_PARTS = 4
 DIMS0 = (((0,), (0,)), ((), ()))
 DIMS1 = (((1,), (1,)), ((), ()))
 
@@ -281,22 +282,25 @@
         soft_mix[step] = rows_out[step * slots : (step + 1) * slots, :].astype(jnp.bfloat16)
 
 
-def roll_kernel(slots, move_dist, move_slot, source, target):
+def roll_kernel(slots, move_dist, move_slot, source, target, metas):
     count = source.shape[0]
+    part = target.shape[0]
     chunk = target.shape[1] // slots
+    begin = pl.program_id(0) * part
+    group = lax.axis_index("grp")
     for slot in range(slots):
         here = slice(slot * chunk, (slot + 1) * chunk)
         distance = distance_of(slot, move_dist, move_slot)
-
-        def step(at, _):
-            target[lax.rem(at + distance, count), here, :] = source[at, here, :]
-            return 0
-
-        lax.fori_loop(0, count, step, 0, unroll=4)
+        for at in range(part):
+            origin = lax.rem(begin + at - distance + count, count)
+            target[at, here, :] = source[origin, here, :]
+        sender = lax.rem(group - distance + count, count)
+        lines = source[sender, slots * chunk :, :].astype(jnp.float32)
+        metas[slot : slot + 1, :] = lines[slot : slot + 1]
 
 
 def unpack_kernel(
-    steps, move_dist, move_slot, metas, landed, keys, values, states, table, lengths
+    steps, metas, landed, keys, values, states, table, lengths
 ):
     slot = pl.program_id(0)
     heads = states.shape[1]
@@ -304,7 +308,6 @@
     kv_rows = per_slot * page_len
     kv_heads = width // LANES
     entries = table.shape[1]
-    group, count = lax.axis_index("grp"), lax.axis_size("grp")
     chunk = landed.shape[1]
     for pages, first in ((keys, 0), (values, kv_heads * kv_rows)):
         for head in range(kv_heads):
@@ -316,9 +319,7 @@
         first = 2 * kv_heads * kv_rows + head * LANES
         for at, place, here in pieces(first, LANES, chunk):
             states[0, head, at : at + 16, :] = landed[place, here : here + 16, :].astype(jnp.float32)
-    source = lax.rem(group - distance_of(slot, move_dist, move_slot) + count, count)
-    meta = metas[source].astype(jnp.float32)
-    meta = jnp.where(slot == 0, meta[0:1], meta[1:2])
+    meta = jnp.where(slot == 0, metas[0:1], metas[1:2])
     row = lax.broadcasted_iota(jnp.int32, table.shape, 0)
     table[...] = jnp.where(row == slot, meta[:, :entries].astype(jnp.int32), table[...])
     lane = lax.broadcasted_iota(jnp.int32, meta.shape, 1)
@@ -331,8 +332,8 @@
     return lax.all_to_all(value, "grp", 0, 0, tiled=True)
 
 
-def by_slot(array, axis, slots):
-    shape = tuple(size // slots if at == axis else size for at, size in enumerate(array.shape))
+def by_part(array, axis, parts):
+    shape = tuple(size // parts if at == axis else size for at, size in enumerate(array.shape))
     return pl.BlockSpec(shape, lambda i: tuple(i if at == axis else 0 for at in range(len(shape))))
 
 
@@ -389,8 +390,8 @@
         ),
         [scalars()] * 3
         + [blocked(new_keys), blocked(new_values)]
-        + [by_slot(key_cache, 2, slots), by_slot(value_cache, 2, slots)]
-        + [blocked(light_k), blocked(light_v), by_slot(light_state, 0, slots)],
+        + [by_part(key_cache, 2, slots), by_part(value_cache, 2, slots)]
+        + [blocked(light_k), blocked(light_v), by_part(light_state, 0, slots)],
         blocked(first_all),
         cost(1 << 24, 7 << 20),
         "pack",
@@ -425,19 +426,23 @@
         [pltpu.VMEM((kv_all, LANES), jnp.bfloat16)] * slots
         + [pltpu.VMEM((rows, queries.shape[2]), jnp.float32)],
     )
+    spread, *sends = lax.optimization_barrier((spread, *sends))
     received = [sends[0]] + [
         lax.ppermute(sends[turn], "tp", [(at, at ^ turn) for at in range(tp_count)])
         for turn in range(1, tp_count)
     ]
 
-    turned = called(
+    meta_all = shape((slots, LANES), jnp.float32)
+    turned, metas = called(
         functools.partial(roll_kernel, slots),
-        send_all,
+        (send_all, meta_all),
         (move_dist, move_slot, spread),
         [scalars()] * 2 + [blocked(first_all)],
-        blocked(send_all),
+        (by_part(send_all, 0, ROLL_PARTS), blocked(meta_all)),
         cost(1 << 10, 5 << 20),
         "roll",
+        grid=ROLL_PARTS,
+        vmem=60,
     )
     landed = exchanged(turned)
 
@@ -459,14 +464,13 @@
         shape(page_table.shape, jnp.int32),
         shape(context.shape, jnp.int32),
     )
-    metas = pl.BlockSpec((groups, META_ROWS, LANES), lambda i: (0, slots * chunk // META_ROWS, 0))
     keys, values, states, table, lengths = called(
         functools.partial(unpack_kernel, steps),
         outs,
-        (move_dist, move_slot, spread, landed),
-        [scalars()] * 2 + [metas, by_slot(send_all, 1, slots)],
+        (metas, landed),
+        [blocked(meta_all), by_part(send_all, 1, slots)],
         (
-            by_slot(outs[0], 2, slots), by_slot(outs[1], 2, slots), by_slot(outs[2], 0, slots),
+            by_part(outs[0], 2, slots), by_part(outs[1], 2, slots), by_part(outs[2], 0, slots),
             blocked(outs[3]), scalars(),
         ),
         cost(1 << 20, 6 << 20),

time: 162 us -> 163 us (level); the launches traced: 159 us -> 162 us
  blocking collectives: 75.1 us -> 0 us
  waiting for transfers between devices: 42.4 us -> 116 us
  starting transfers between devices: 18.7 us -> 25.9 us
  local copies, waits for them, and re-layouts: 5.42 us -> 1.65 us
    all_to_all x1 -> x0, blocking collectives: 75.1 us -> none  [exchanged(): return lax.all_to_all(value, 'grp', 0, 0, tiled=True)]
    all_to_all x1 -> x2, waiting for transfers between devices: 1.17 us -> 65.5 us  [exchanged(): return lax.all_to_all(value, 'grp', 0, 0, tiled=True)]
    all_to_all x1 -> x2, starting transfers between devices: 12.2 us -> 24 us  [exchanged(): return lax.all_to_all(value, 'grp', 0, 0, tiled=True)]
    ppermute x3, waiting for transfers between devices: 41.2 us -> 50.7 us  [per_device(): lax.ppermute(sends[turn], 'tp', [(at, at ^ turn) for at in range(tp_count)])]
    ppermute x3, starting transfers between devices: 6.47 us -> 1.96 us  [per_device(): lax.ppermute(sends[turn], 'tp', [(at, at ^ turn) for at in range(tp_count)])]
    unnamed x30 -> x26, local copies, waits for them, and re-layouts: 5.42 us -> 1.65 us
  transfers between devices with their start and end apart: 4 -> 5, of which waited for: 3 -> 4; matrix products, arithmetic and copies ran while one was open for 0% -> 0% of each run, Pallas kernels for 4% -> 4%
where the time goes in v1:
time: 163 us; the launch traced here: 162 us
  waiting for transfers between devices  116 us (71%)
  starting transfers between devices  25.9 us (16%)
  Pallas kernels  17.4 us (11%)
  local copies, waits for them, and re-layouts  1.65 us (1%)
    all_to_all x2, waiting for transfers between devices, exchanged(): return lax.all_to_all(value, 'grp', 0, 0, tiled=True)  65.5 us
    ppermute x3, waiting for transfers between devices, per_device(): lax.ppermute(sends[turn], 'tp', [(at, at ^ turn) for at in range(tp_count)])  50.7 us
    all_to_all x2, starting transfers between devices, exchanged(): return lax.all_to_all(value, 'grp', 0, 0, tiled=True)  24 us
    pallas_call x6, Pallas kernels, called(): pl.pallas_call(kernel, grid=(grid,), out_shape=out_shape, in_specs=in_spe...  17.4 us
  transfers between devices with their start and end apart: 5, of which 4 were waited for; matrix products, arithmetic and copies ran while one was open for 0% of the time, Pallas kernels for 4%

profile of v1, /device:TPU:8, one launch (start us, length us, event | category | flops | bytes accessed | tf_op | source)
XLA Modules:
  0.0 162.0 jit_solution(17146172493247930354)
XLA Ops:
  0.6 4.3 %pack.1 = bf16[64,168,128]{2,1,0:T(8,128)(2,1)} custom-call(s32[2,12]{1,0:T(2,128)} %table.3, s32[2]{0:T(128)} %context.3, f32[16]{0:T(128)} %decay.3, bf16[4,2,1024]{2,1,0:T(2,128)(2,1)} %new_keys.3, bf16[4,2,1024]{2,1,0:T(2,128)(2,1)} %new_values.3, bf16[1,1,6,64,1024]{4,3,2,1,0:T(8,128)(2,1)} %key_cache.3, bf16[1,1,6,64,1024]{4,3,2,1,0:T(8,128)(2,1)} %value_cache.3, ...), custom_call_target="tpu_custom_call" | custom-call | flops 16777216 | bytes 7340032 | tf_op jit(solution)/shard_map/pack/pallas_call | solution.py:341
  5.0 0.0 copy-start.5
  5.0 0.0 copy-start.6
  5.0 0.0 copy-start.7
  5.0 0.0 copy-start.9
  5.0 0.0 copy-start.10
  5.0 15.4 %all-to-all-start = ((bf16[64,168,128]{2,1,0:T(8,128)(2,1)}), bf16[64,168,128]{2,1,0:T(8,128)(2,1)}, u32[]{:S(2)}, u32[]{:S(2)}) async-start(bf16[64,168,128]{2,1,0:T(8,128)(2,1)} %pack.1), calls=%async_computation | async-start | bytes 5505024 | tf_op jit(solution)/shard_map/all_to_all | solution.py:332
  20.5 3.3 %attend.1 = (bf16[128,256]{1,0:T(8,128)(2,1)S(1)}, bf16[128,256]{1,0:T(8,128)(2,1)S(1)}, bf16[128,256]{1,0:T(8,128)(2,1)S(1)}, bf16[128,256]{1,0:T(8,128)(2,1)S(1)}) custom-call(s32[2,12]{1,0:T(2,128)S(1)} %copy-done.9, s32[2]{0:T(128)S(1)} %copy-done.10, bf16[4,2,8192]{2,1,0:T(2,128)(2,1)S(1)} %copy-done.5, bf16[4,2,1024]{2,1,0:T(2,128)(2,1)S(1)} %copy-done.6, ...), custom_call_target="tpu_custom_call" | custom-call | flops 268435456 | bytes 2097152 | tf_op jit(solution)/shard_map/attend/pallas_call | solution.py:341
  23.8 60.7 %all-to-all-done.source = bf16[64,168,128]{2,1,0:T(8,128)(2,1)} async-done(((bf16[64,168,128]{2,1,0:T(8,128)(2,1)}), bf16[64,168,128]{2,1,0:T(8,128)(2,1)}, u32[]{:S(2)}, u32[]{:S(2)}) %all-to-all-start) | async-done | bytes 2752544 | tf_op jit(solution)/shard_map/all_to_all | solution.py:332
  84.5 4.0 %roll.1 = (bf16[64,160,128]{2,1,0:T(8,128)(2,1)}, f32[2,128]{1,0:T(2,128)}) custom-call(s32[2]{0:T(128)} %move_dist.1, s32[2]{0:T(128)} %move_slot.1, bf16[64,168,128]{2,1,0:T(8,128)(2,1)} %all-to-all-done.source), custom_call_target="tpu_custom_call" | custom-call | flops 1024 | bytes 5242880 | tf_op jit(solution)/shard_map/roll/pallas_call | solution.py:341
  88.5 0.0 copy-start.11
  88.5 0.0 copy-start.12
  88.5 8.6 %all-to-all-start.1 = ((bf16[64,160,128]{2,1,0:T(8,128)(2,1)}), bf16[64,160,128]{2,1,0:T(8,128)(2,1)S(1)}, u32[]{:S(2)}, u32[]{:S(2)}) async-start(bf16[64,160,128]{2,1,0:T(8,128)(2,1)} %get-tuple-element.33), calls=%async_computation.1 | async-start | bytes 5242880 | tf_op jit(solution)/shard_map/all_to_all | solution.py:332
  97.1 0.1 collective-permute-start
  97.2 1.7 %collective-permute-start.1 = (bf16[128,256]{1,0:T(8,128)(2,1)S(1)}, bf16[128,256]{1,0:T(8,128)(2,1)S(1)}, u32[]{:S(2)}, u32[]{:S(2)}) collective-permute-start(bf16[128,256]{1,0:T(8,128)(2,1)S(1)} %get-tuple-element.29), channel_id=1, source_target_pairs={{0,2},{1,3},{2,0},{3,1},{4,6},{5,7},{6,4},{7,5},{8,10},{9,11},{10,... | collective-permute-start | bytes 196616 | tf_op jit(solution)/shard_map/ppermute | solution.py:431
  98.8 0.2 collective-permute-start.2
  99.0 0.0 copy-start
  99.1 1.6 copy-done
  100.6 2.4 %linear.1 = bf16[4,2,2048]{2,1,0:T(2,128)(2,1)} custom-call(f32[16]{0:T(128)S(1)} %copy-done.11, bf16[4,2,2048]{2,1,0:T(2,128)(2,1)S(1)} %copy-done.8, bf16[4,2,2048]{2,1,0:T(2,128)(2,1)S(1)} %copy-done.3, bf16[4,2,2048]{2,1,0:T(2,128)(2,1)S(1)} %copy-done.4, f32[2,16,128,128]{3,2,1,0:T(8,128)S(1)} %copy-done), custom_call_target="tpu_custom_call" | custom-call | flops 16777216 | bytes 3145728 | tf_op jit(solution)/shard_map/linear/pallas_call | solution.py:341
  103.1 49.7 %collective-permute-done.1.refs_2_ = bf16[128,256]{1,0:T(8,128)(2,1)S(1)} collective-permute-done((bf16[128,256]{1,0:T(8,128)(2,1)S(1)}, bf16[128,256]{1,0:T(8,128)(2,1)S(1)}, u32[]{:S(2)}, u32[]{:S(2)}) %collective-permute-start.1) | collective-permute-done | bytes 65568 | tf_op jit(solution)/shard_map/ppermute | solution.py:431
  152.7 1.1 collective-permute-done.2.refs_3_
  153.8 1.1 merge.1
  154.8 4.9 %all-to-all-done.1.landed = bf16[64,160,128]{2,1,0:T(8,128)(2,1)S(1)} async-done(((bf16[64,160,128]{2,1,0:T(8,128)(2,1)}), bf16[64,160,128]{2,1,0:T(8,128)(2,1)S(1)}, u32[]{:S(2)}, u32[]{:S(2)}) %all-to-all-start.1) | async-done | bytes 2621472 | tf_op jit(solution)/shard_map/all_to_all | solution.py:332
  159.7 2.3 %unpack.1 = (bf16[1,1,6,64,1024]{4,3,2,1,0:T(8,128)(2,1)}, bf16[1,1,6,64,1024]{4,3,2,1,0:T(8,128)(2,1)}, f32[2,16,128,128]{3,2,1,0:T(8,128)}, s32[2,12]{1,0:T(2,128)}, s32[2]{0:T(128)}) custom-call(f32[2,128]{1,0:T(2,128)S(1)} %copy-done.12, bf16[64,160,128]{2,1,0:T(8,128)(2,1)S(1)} %all-to-all-done.1.landed), custom_call_target="tpu_custom_call" | custom-call | flops 1048576 | bytes 6291456 | tf_op jit(solution)/shard_map/unpack/pallas_call | solution.py:341
  (18 shorter events, 0.0 us)
Async XLA Ops:
  5.0 15.5 %copy-start.1 = (bf16[1,1,6,64,1024]{4,3,2,1,0:T(8,128)(2,1)S(1)}, bf16[1,1,6,64,1024]{4,3,2,1,0:T(8,128)(2,1)}, u32[]{:S(2)}) copy-start(bf16[1,1,6,64,1024]{4,3,2,1,0:T(8,128)(2,1)} %key_cache.3) | copy-start | bytes 2359300
  5.0 15.5 %copy-start.2 = (bf16[1,1,6,64,1024]{4,3,2,1,0:T(8,128)(2,1)S(1)}, bf16[1,1,6,64,1024]{4,3,2,1,0:T(8,128)(2,1)}, u32[]{:S(2)}) copy-start(bf16[1,1,6,64,1024]{4,3,2,1,0:T(8,128)(2,1)} %value_cache.3) | copy-start | bytes 2359300
  5.0 15.5 %copy-start.5 = (bf16[4,2,8192]{2,1,0:T(2,128)(2,1)S(1)}, bf16[4,2,8192]{2,1,0:T(2,128)(2,1)}, u32[]{:S(2)}) copy-start(bf16[4,2,8192]{2,1,0:T(2,128)(2,1)} %queries.1) | copy-start | bytes 393220
  5.0 15.5 %copy-start.6 = (bf16[4,2,1024]{2,1,0:T(2,128)(2,1)S(1)}, bf16[4,2,1024]{2,1,0:T(2,128)(2,1)}, u32[]{:S(2)}) copy-start(bf16[4,2,1024]{2,1,0:T(2,128)(2,1)} %new_keys.3) | copy-start | bytes 49156
  5.0 15.5 %copy-start.7 = (bf16[4,2,1024]{2,1,0:T(2,128)(2,1)S(1)}, bf16[4,2,1024]{2,1,0:T(2,128)(2,1)}, u32[]{:S(2)}) copy-start(bf16[4,2,1024]{2,1,0:T(2,128)(2,1)} %new_values.3) | copy-start | bytes 49156
  5.0 15.5 %copy-start.9 = (s32[2,12]{1,0:T(2,128)S(1)}, s32[2,12]{1,0:T(2,128)}, u32[]{:S(2)}) copy-start(s32[2,12]{1,0:T(2,128)} %table.3) | copy-start | bytes 292
  5.0 15.5 %copy-start.10 = (s32[2]{0:T(128)S(1)}, s32[2]{0:T(128)}, u32[]{:S(2)}) copy-start(s32[2]{0:T(128)} %context.3) | copy-start | bytes 28
  5.0 79.5 %all-to-all-start = ((bf16[64,168,128]{2,1,0:T(8,128)(2,1)}), bf16[64,168,128]{2,1,0:T(8,128)(2,1)}, u32[]{:S(2)}, u32[]{:S(2)}) async-start(bf16[64,168,128]{2,1,0:T(8,128)(2,1)} %pack.1), calls=%async_computation | async-start | bytes 5505024 | tf_op jit(solution)/shard_map/all_to_all | solution.py:332
  88.5 10.6 %copy-start.3 = (bf16[4,2,2048]{2,1,0:T(2,128)(2,1)S(1)}, bf16[4,2,2048]{2,1,0:T(2,128)(2,1)}, u32[]{:S(2)}) copy-start(bf16[4,2,2048]{2,1,0:T(2,128)(2,1)} %light_k.3) | copy-start | bytes 98308
  88.5 10.6 %copy-start.4 = (bf16[4,2,2048]{2,1,0:T(2,128)(2,1)S(1)}, bf16[4,2,2048]{2,1,0:T(2,128)(2,1)}, u32[]{:S(2)}) copy-start(bf16[4,2,2048]{2,1,0:T(2,128)(2,1)} %light_v.3) | copy-start | bytes 98308
  88.5 10.6 %copy-start.8 = (bf16[4,2,2048]{2,1,0:T(2,128)(2,1)S(1)}, bf16[4,2,2048]{2,1,0:T(2,128)(2,1)}, u32[]{:S(2)}) copy-start(bf16[4,2,2048]{2,1,0:T(2,128)(2,1)} %light_q.1) | copy-start | bytes 98308
  88.5 10.6 %copy-start.11 = (f32[16]{0:T(128)S(1)}, f32[16]{0:T(128)}, u32[]{:S(2)}) copy-start(f32[16]{0:T(128)} %decay.3) | copy-start | bytes 196
  88.5 71.2 %copy-start.12 = (f32[2,128]{1,0:T(2,128)S(1)}, f32[2,128]{1,0:T(2,128)}, u32[]{:S(2)}) copy-start(f32[2,128]{1,0:T(2,128)} %get-tuple-element.32.metas) | copy-start | bytes 3076
  88.5 71.2 %all-to-all-start.1 = ((bf16[64,160,128]{2,1,0:T(8,128)(2,1)}), bf16[64,160,128]{2,1,0:T(8,128)(2,1)S(1)}, u32[]{:S(2)}, u32[]{:S(2)}) async-start(bf16[64,160,128]{2,1,0:T(8,128)(2,1)} %get-tuple-element.33), calls=%async_computation.1 | async-start | bytes 5242880 | tf_op jit(solution)/shard_map/all_to_all | solution.py:332
  97.1 6.0 %collective-permute-start = (bf16[128,256]{1,0:T(8,128)(2,1)S(1)}, bf16[128,256]{1,0:T(8,128)(2,1)S(1)}, u32[]{:S(2)}, u32[]{:S(2)}) collective-permute-start(bf16[128,256]{1,0:T(8,128)(2,1)S(1)} %get-tuple-element.28), channel_id=1, source_target_pairs={{0,1},{1,0},{2,3},{3,2},{4,5},{5,4},{6,7},{7,6},{8,9},{9,8},{10,11... | collective-permute-start | bytes 196616 | tf_op jit(solution)/shard_map/ppermute | solution.py:431
  97.2 55.5 %collective-permute-start.1 = (bf16[128,256]{1,0:T(8,128)(2,1)S(1)}, bf16[128,256]{1,0:T(8,128)(2,1)S(1)}, u32[]{:S(2)}, u32[]{:S(2)}) collective-permute-start(bf16[128,256]{1,0:T(8,128)(2,1)S(1)} %get-tuple-element.29), channel_id=1, source_target_pairs={{0,2},{1,3},{2,0},{3,1},{4,6},{5,7},{6,4},{7,5},{8,10},{9,11},{10,... | collective-permute-start | bytes 196616 | tf_op jit(solution)/shard_map/ppermute | solution.py:431
  98.8 55.0 %collective-permute-start.2 = (bf16[128,256]{1,0:T(8,128)(2,1)S(1)}, bf16[128,256]{1,0:T(8,128)(2,1)S(1)}, u32[]{:S(2)}, u32[]{:S(2)}) collective-permute-start(bf16[128,256]{1,0:T(8,128)(2,1)S(1)} %get-tuple-element.30), channel_id=1, source_target_pairs={{0,3},{1,2},{2,1},{3,0},{4,7},{5,6},{6,5},{7,4},{8,11},{9,10},{10,... | collective-permute-start | bytes 196616 | tf_op jit(solution)/shard_map/ppermute | solution.py:431
  99.0 1.6 copy-start
